TPU v7x, 32 devices: a whole 2x2x4 slice. The times are simulated.
32 devices in a mesh: grp: 2 (over y), row: 4 (over x, core), col: 4 (over z).
Axes of the slice: x: 2, y: 2, z: 4, core: 2. Of those that a mesh axis runs over, the one named last changes fastest.
Arguments:
- root_inverse: float32 [4096, 2048], P(('grp', 'row'), 'col'), parts along dimension 0, may hold values from -1 to 4, as said below
- panel: float32 [4096, 2048], P(('grp', 'row'), 'col'), parts along dimension 0, may hold values from -0.125 to 0.125
- node_inverse: float32 [4096, 2048], P(('grp', 'row'), 'col'), parts along dimension 0, may hold values from -1 to 4, as said below
- structure: int32 [64], P(('grp', 'row')), parts along dimension 0, may hold values 0 or 1
Outputs:
- sigma_root: float32 [4096, 2048], P(('grp', 'row'), 'col'), parts along dimension 0
- sigma_off: float32 [4096, 2048], P(('grp', 'row'), 'col'), parts along dimension 0
- sigma_node: float32 [4096, 2048], P(('grp', 'row'), 'col'), parts along dimension 0
There are 2 independent parts, one for each index of `grp`. A program takes and returns all parts, laid end to end along the dimension named above; each array names one. Nothing has to cross between parts.
Inputs may be any that keep to these rules, and one draw needn't show every extreme that they name: `root_inverse`: lower triangular, diagonal entries 1 or more. `node_inverse`: lower triangular, diagonal entries 1 or more.
All inputs are finite; a program needn't handle non-finite values. No bound on the sum of `structure` on one device may be relied on, other than what follows from the above.
Results may differ from a plain program's by a relative error of at most 0.000098.
Values sent between devices are 32-bit elements; how exact they have to be, the bound alone decides.
A program may use at most 128 MiB of HBM per device.

v0:
```python
import jax
import jax.numpy as jnp
from jax import lax
from jax.sharding import PartitionSpec as P

BS = 64


PRECISE = lax.Precision.HIGHEST


def product(left_side, right_side):
    return jnp.dot(left_side, right_side, precision=PRECISE, preferred_element_type=jnp.float32)


def shards(root_inverse, panel, node_inverse, structure):
    local_rows = root_inverse.shape[0]
    node_local_cols = node_inverse.shape[1]
    root_rows = lax.all_gather(root_inverse, "col", axis=1, tiled=True)
    segment = root_rows
    sigma_root = lax.psum_scatter(
        product(segment.T, root_inverse), "row", scatter_dimension=0, tiled=True
    )
    row_mask = jnp.repeat(structure, BS).astype(jnp.float32)
    masked = panel * row_mask[:, None]
    panel_full, node_rows = (
        lax.all_gather(masked, "col", axis=1, tiled=True),
        lax.all_gather(node_inverse, "col", axis=1, tiled=True),
    )
    segment = panel_full
    scaled = product(segment, lax.all_gather(node_inverse, "row", axis=0, tiled=True))
    scaled_cols = lax.all_gather(scaled, "row", axis=0, tiled=True)
    segment = scaled_cols
    sigma_off = jnp.zeros((local_rows, node_local_cols), jnp.float32) - product(
        lax.all_gather(sigma_root, "col", axis=1, tiled=True), segment
    )
    scaled_full = lax.all_gather(scaled, "col", axis=1, tiled=True)
    sigma_node = lax.psum_scatter(
        product(node_rows.T, node_inverse) - product(scaled_full.T, sigma_off),
        "row",
        scatter_dimension=0,
        tiled=True,
    )
    return (sigma_root, sigma_off, sigma_node)


def solution(mesh):
    placed = (
        P(("grp", "row"), "col"),
        P(("grp", "row"), "col"),
        P(("grp", "row"), "col"),
        P(("grp", "row")),
    )
    return jax.shard_map(
        shards,
        mesh=mesh,
        in_specs=placed,
        out_specs=(P(("grp", "row"), "col"), P(("grp", "row"), "col"), P(("grp", "row"), "col")),
        check_vma=False,
    )
```

profile of v0, /device:TPU:26, one launch (start us, length us, event | category | flops | bytes accessed | tf_op | source)
XLA Modules:
  0.0 596.2 jit_solution(1038044514650494239)
XLA Ops:
  7.2 0.0 all-gather.8.cloned.1.call-start
  7.2 0.7 all-gather.8.cloned.1.call-update
  7.9 0.0 all-gather.12.cloned.1.call-start
  8.0 0.7 convert_element_type.11
  8.6 0.1 broadcast_in_dim.8
  8.7 0.1 convert_element_type.12
  8.8 2.3 broadcast_multiply_fusion
  11.1 0.0 all-gather.14.cloned.1.call-start
  11.2 0.7 all-gather.14.cloned.1.call-update
  11.9 0.0 reduce-scatter.3.cloned.1.call-start
  11.9 76.9 %all-gather.8.cloned.1.call-done = f32[512,2048]{1,0:T(8,128)} async-done(((f32[512,512]{1,0:T(8,128)}), f32[512,2048]{1,0:T(8,128)}) %all-gather.8.cloned.1.call-update) | async-done | bytes 4194320 | tf_op jit(solution)/shard_map/all_gather | solution.py:19
  88.8 9.9 %fusion = f32[2048,512]{1,0:T(8,128)} fusion(f32[512,2048]{1,0:T(8,128)} %all-gather.8.cloned.1.call-done, f32[512,512]{1,0:T(8,128)S(1)} %copy-done.2), kind=kOutput, calls=%fused_computation.3 | convolution fusion | flops 6442450944 | bytes 9437184 | tf_op jit(solution)/shard_map/dot_general | solution.py:13
  98.8 0.0 all-gather.18.cloned.1.call-start
  98.8 0.5 all-gather.18.cloned.1.call-update
  99.4 0.0 all-gather.16.cloned.1.call-start
  99.4 70.9 %all-gather.12.cloned.1.call-done = f32[512,2048]{1,0:T(8,128)} async-done(((f32[512,512]{1,0:T(8,128)}), f32[512,2048]{1,0:T(8,128)}) %all-gather.12.cloned.1.call-update) | async-done | bytes 4194320 | tf_op jit(solution)/shard_map/all_gather | solution.py:27
  170.3 36.2 %all-gather.14.cloned.1.call-done = f32[2048,512]{1,0:T(8,128)} async-done(((f32[512,512]{1,0:T(8,128)}), f32[2048,512]{1,0:T(8,128)}) %all-gather.14.cloned.1.call-update) | async-done | bytes 4194320 | tf_op jit(solution)/shard_map/all_gather | solution.py:31
  206.5 10.2 %fusion.1 = f32[512,512]{1,0:T(8,128)} fusion(f32[512,2048]{1,0:T(8,128)} %all-gather.12.cloned.1.call-done, f32[2048,512]{1,0:T(8,128)} %all-gather.14.cloned.1.call-done), kind=kOutput, calls=%fused_computation.4 | convolution fusion | flops 6442450944 | bytes 9437184 | tf_op jit(solution)/shard_map/dot_general | solution.py:13
  216.7 0.0 all-gather.10.cloned.1.call-start
  216.8 37.2 %reduce-scatter.3.cloned.1.call-done = f32[512,512]{1,0:T(8,128)} async-done(((f32[2048,512]{1,0:T(8,128)}), f32[512,512]{1,0:T(8,128)}) %reduce-scatter.3.cloned.1.call-update) | async-done | bytes 1048592 | tf_op jit(solution)/shard_map/reduce_scatter | solution.py:21
  254.0 0.0 all-gather.20.cloned.1.call-start
  254.1 0.7 all-gather.20.cloned.1.call-update
  254.8 0.2 reduce-scatter.5.cloned.1.call-start
  255.0 79.7 %all-gather.18.cloned.1.call-done = f32[512,2048]{1,0:T(8,128)} async-done(((f32[512,512]{1,0:T(8,128)}), f32[512,2048]{1,0:T(8,128)}) %all-gather.18.cloned.1.call-update) | async-done | bytes 4194320 | tf_op jit(solution)/shard_map/all_gather | solution.py:28
  334.7 9.8 %fusion.2 = f32[2048,512]{1,0:T(8,128)} fusion(f32[512,2048]{1,0:T(8,128)} %all-gather.18.cloned.1.call-done, f32[512,512]{1,0:T(8,128)S(1)} %copy-done), kind=kOutput, calls=%fused_computation.5 | convolution fusion | flops 6442450944 | bytes 9437184 | tf_op jit(solution)/shard_map/dot_general | solution.py:13
  344.5 26.9 %all-gather.16.cloned.1.call-done = f32[2048,512]{1,0:T(8,128)} async-done(((f32[512,512]{1,0:T(8,128)}), f32[2048,512]{1,0:T(8,128)}) %all-gather.16.cloned.1.call-update) | async-done | bytes 4194320 | tf_op jit(solution)/shard_map/all_gather | solution.py:32
  371.4 81.4 %all-gather.10.cloned.1.call-done = f32[512,2048]{1,0:T(8,128)} async-done(((f32[512,512]{1,0:T(8,128)}), f32[512,2048]{1,0:T(8,128)}) %all-gather.10.cloned.1.call-update) | async-done | bytes 4194320 | tf_op jit(solution)/shard_map/all_gather | solution.py:35
  452.8 9.3 %convolution_subtract_fusion.1 = f32[512,512]{1,0:T(8,128)S(1)} fusion(f32[512,2048]{1,0:T(8,128)} %all-gather.10.cloned.1.call-done, f32[2048,512]{1,0:T(8,128)} %all-gather.16.cloned.1.call-done), kind=kOutput, calls=%fused_computation.1 | convolution fusion | flops 6442713088 | bytes 9437184 | tf_op jit(solution)/shard_map/dot_general | solution.py:13
  462.2 72.2 %all-gather.20.cloned.1.call-done = f32[512,2048]{1,0:T(8,128)} async-done(((f32[512,512]{1,0:T(8,128)}), f32[512,2048]{1,0:T(8,128)}) %all-gather.20.cloned.1.call-update) | async-done | bytes 4194320 | tf_op jit(solution)/shard_map/all_gather | solution.py:37
  534.4 10.5 %convolution_subtract_fusion = f32[2048,512]{1,0:T(8,128)} fusion(f32[2048,512]{1,0:T(8,128)} %fusion.2, f32[512,2048]{1,0:T(8,128)} %all-gather.20.cloned.1.call-done, f32[512,512]{1,0:T(8,128)S(1)} %convolution_subtract_fusion.1), kind=kOutput, calls=%fused_computation | convolution fusion | flops 6443499520 | bytes 13631488 | tf_op jit(solution)/shard_map/dot_general | solution.py:13
  544.9 0.0 reduce-scatter.5.cloned.1.call-update
  544.9 44.8 %reduce-scatter.5.cloned.1.call-done = f32[512,512]{1,0:T(8,128)} async-done(((f32[2048,512]{1,0:T(8,128)}), f32[512,512]{1,0:T(8,128)}) %reduce-scatter.5.cloned.1.call-update) | async-done | bytes 1048592 | tf_op jit(solution)/shard_map/reduce_scatter | solution.py:38
  (10 shorter events, 0.1 us)
Async XLA Ops:
  7.2 81.7 %copy-start.2 = (f32[512,512]{1,0:T(8,128)S(1)}, f32[512,512]{1,0:T(8,128)}, u32[]{:S(2)}) copy-start(f32[512,512]{1,0:T(8,128)} %param.4) | copy-start | bytes 3145732
  7.2 81.7 %all-gather.8.cloned.1.call-start = ((), (), s32[]{:S(2)}) async-start(), calls=%async_computation.2 | async-start | bytes 5242880 | tf_op jit(solution)/shard_map/all_gather | solution.py:19
  7.9 162.4 %all-gather.12.cloned.1.call-start = ((), (), s32[]{:S(2)}) async-start(), calls=%async_computation.5 | async-start | bytes 5242880 | tf_op jit(solution)/shard_map/all_gather | solution.py:27
  11.1 195.4 %all-gather.14.cloned.1.call-start = ((), (), s32[]{:S(2)}) async-start(), calls=%async_computation.6 | async-start | bytes 5242880 | tf_op jit(solution)/shard_map/all_gather | solution.py:31
  11.9 242.1 %reduce-scatter.3.cloned.1.call-start = ((), (), s32[]{:S(2)}) async-start(), calls=%async_computation.3 | async-start | bytes 5242880 | tf_op jit(solution)/shard_map/reduce_scatter | solution.py:21
  98.8 236.0 %all-gather.18.cloned.1.call-start = ((), (), s32[]{:S(2)}) async-start(), calls=%async_computation.8 | async-start | bytes 5242880 | tf_op jit(solution)/shard_map/all_gather | solution.py:28
  99.3 235.4 %copy-start = (f32[512,512]{1,0:T(8,128)S(1)}, f32[512,512]{1,0:T(8,128)}, u32[]{:S(2)}) copy-start(f32[512,512]{1,0:T(8,128)} %param.6) | copy-start | bytes 3145732
  99.4 272.0 %all-gather.16.cloned.1.call-start = ((), (), s32[]{:S(2)}) async-start(), calls=%async_computation.7 | async-start | bytes 5242880 | tf_op jit(solution)/shard_map/all_gather | solution.py:32
  216.7 236.1 %all-gather.10.cloned.1.call-start = ((), (), s32[]{:S(2)}) async-start(), calls=%async_computation.4 | async-start | bytes 5242880 | tf_op jit(solution)/shard_map/all_gather | solution.py:35
  254.0 280.4 %all-gather.20.cloned.1.call-start = ((), (), s32[]{:S(2)}) async-start(), calls=%async_computation.9 | async-start | bytes 5242880 | tf_op jit(solution)/shard_map/all_gather | solution.py:37
  254.8 334.9 %reduce-scatter.5.cloned.1.call-start = ((), (), s32[]{:S(2)}) async-start(), calls=%async_computation.10 | async-start | bytes 5242880 | tf_op jit(solution)/shard_map/reduce_scatter | solution.py:38
  462.2 82.7 %copy-start.1 = (f32[512,512]{1,0:T(8,128)}, f32[512,512]{1,0:T(8,128)S(1)}, u32[]{:S(2)}) copy-start(f32[512,512]{1,0:T(8,128)S(1)} %convolution_subtract_fusion.1) | copy-start | bytes 3145732
Sparse Core Ops, SparseCore 0:
  9.6 79.2 all-gather.7
  91.0 79.2 all-gather.11
  171.9 34.5 all-gather.13
  209.4 44.4 reduce-scatter.2
  255.5 79.1 all-gather.17
  336.8 34.5 all-gather.15
  373.6 79.1 all-gather.9
  455.1 79.2 all-gather.19
  545.0 44.5 reduce-scatter.4
where the time goes:
time: 599 us; the launch traced here: 596 us
  waiting for transfers between devices  529 us (88%)
  matrix products  49.7 us (8%)
  between operations  13.9 us (2%)
    all_gather x1, waiting for transfers between devices, shards(): lax.all_gather(sigma_root, 'col', axis=1, tiled=True)  81.4 us
    all_gather x1, waiting for transfers between devices, shards(): lax.all_gather(node_inverse, 'col', axis=1, tiled=True)  79.7 us
    all_gather x1, waiting for transfers between devices, shards(): root_rows = lax.all_gather(root_inverse, 'col', axis=1, tiled=True)  76.9 us
    all_gather x1, waiting for transfers between devices, shards(): scaled_full = lax.all_gather(scaled, 'col', axis=1, tiled=True)  72.2 us
    all_gather x1, waiting for transfers between devices, shards(): lax.all_gather(masked, 'col', axis=1, tiled=True)  70.9 us
    dot_general x5, matrix products, product(): jnp.dot(left_side, right_side, precision=PRECISE, preferred_element_type=...  49.7 us
    reduce_scatter x1, waiting for transfers between devices, shards(): lax.psum_scatter(product(node_rows.T, node_inverse) - product(scaled_full...  44.8 us
    reduce_scatter x1, waiting for transfers between devices, shards(): lax.psum_scatter(product(segment.T, root_inverse), 'row', scatter_dimensi...  37.2 us
  transfers between devices with their start and end apart: 9, of which 9 were waited for; matrix products, arithmetic and copies ran while one was open for 7% of the time, Pallas kernels for 0%

commit v1 on v0

v1 whole, which is shorter than its diff:
```python
import functools

import jax
import jax.numpy as jnp
from jax import lax
from jax.experimental import pallas as pl
from jax.experimental.pallas import tpu as pltpu
from jax.sharding import PartitionSpec as P

BS = 64
MESH = pl.DeviceIdType.MESH
F32, BF16 = jnp.float32, jnp.bfloat16


def halves(v):
    high = v.astype(BF16)
    return high, (v - high.astype(F32)).astype(BF16)


def multiply(dst, a, b, transposed, add):
    order = dst.shape[1]
    tile = min(256, order)
    dims = (((0 if transposed else 1,), (0,)), ((), ()))

    def dot(u, v):
        return lax.dot_general(u, v, dims, preferred_element_type=F32)

    def body(t, carry):
        cols = pl.ds(pl.multiple_of(t * tile, tile), tile)
        ah, al = halves(a[...])
        bh, bl = halves(b[:, cols])
        r = dot(ah, bh) + (dot(ah, bl) + dot(al, bh))
        if add:
            r = dst[:, cols] + r
        dst[:, cols] = r
        return carry

    lax.fori_loop(0, order // tile, body, 0)


def kernel(R, C, root, panel, node, mask, out_rr, out_or, out_nn,
           Mb, Rb, Nr, Nc, Xc, Yb, S, A, T1, T2,
           m_s, m_r, r_s, r_r, n_s, n_r, y_s, y_r,
           c_x, c_p, c_r, x_x, x_p, x_r, s1, q1, s2, q2):
    X = R // 2
    i, j = lax.axis_index("row"), lax.axis_index("col")
    x, c = i // 2, lax.rem(i, 2)
    mate = 2 * x + 1 - c
    left, right = lax.rem(j + C - 1, C), lax.rem(j + 1, C)
    k = R - 1 - i

    def copy(src, dst, ssem, rsem, row=None, col=None):
        device = {"row": i if row is None else row, "col": j if col is None else col}
        return pltpu.make_async_remote_copy(
            src_ref=src, dst_ref=dst, send_sem=ssem, recv_sem=rsem,
            device_id=device, device_id_type=MESH)

    def loop(low, high, body):
        def step(t, carry):
            body(t)
            return carry
        lax.fori_loop(low, high, step, 0)

    def when(*conditions):
        both = conditions[0]
        for condition in conditions[1:]:
            both = jnp.logical_and(both, condition)
        return pl.when(both)

    barrier = pltpu.get_barrier_semaphore()

    def greet(row, col):
        pl.semaphore_signal(barrier, inc=1, device_id={"row": row, "col": col}, device_id_type=MESH)

    @pl.when(j > 0)
    def _():
        greet(i, j - 1)

    @pl.when(j < C - 1)
    def _():
        greet(i, j + 1)

    greet(mate, j)
    loop(1, X, lambda d: greet(2 * lax.rem(x + d, X) + c, j))
    pl.semaphore_wait(barrier, X + jnp.where(j > 0, 1, 0) + jnp.where(j < C - 1, 1, 0))

    def to_left(buf, sends, arrivals, l):
        return copy(buf.at[l], buf.at[l], sends.at[0, l], arrivals.at[l], col=left)

    def to_right(buf, sends, arrivals, l):
        return copy(buf.at[l], buf.at[l], sends.at[1, l], arrivals.at[l], col=right)

    def pass_on(buf, sends, arrivals, r, top, end, go_right):
        l = j + r

        @when(l <= top, l < C, j <= end)
        def _():
            if not (isinstance(r, int) and r == 0):
                to_left(buf, sends, arrivals, l).wait_recv()

            @pl.when(j > 0)
            def _():
                to_left(buf, sends, arrivals, l).start()

        if go_right:
            m = j - r

            @when(m >= 0, m <= top, j <= end)
            def _():
                if not (isinstance(r, int) and r == 0):
                    to_left(buf, sends, arrivals, m).wait_recv()

                @when(j < C - 1, j < end)
                def _():
                    to_right(buf, sends, arrivals, m).start()

    def sent_on(buf, sends, arrivals, top, end, go_right):
        def body(r):
            l, m = j + r, j - r

            @when(l <= top, l < C, j <= end, j > 0)
            def _():
                to_left(buf, sends, arrivals, l).wait_send()

            if go_right:
                @when(m >= 0, m <= top, j <= end, j < C - 1, j < end)
                def _():
                    to_right(buf, sends, arrivals, m).wait_send()
        loop(0, C, body)

    def across(buf, sems, arrivals, d_chip):
        return copy(buf.at[i], buf.at[i], sems.at[d_chip], arrivals.at[i], row=2 * d_chip + c)

    def over(buf, sems, arrivals, l):
        return copy(buf.at[l], buf.at[l], sems.at[l], arrivals.at[l], row=mate)

    def spread(buf, xs, ps, arrivals, cross, own):
        def body(d):
            chip = lax.rem(x + d, X)

            @pl.when(cross(i, x, chip))
            def _():
                across(buf, xs, arrivals, chip).start()
        loop(1, X, body)

        @pl.when(own(i))
        def _():
            over(buf, ps, arrivals, i).start()

    def collect(buf, xs, ps, arrivals, cross, own):
        def body(d):
            chip = lax.rem(x + X - d, X)
            l = 2 * chip + c

            @pl.when(cross(l, chip, x))
            def _():
                over(buf, ps, arrivals, l).wait_recv()
                over(buf, ps, arrivals, l).start()
        loop(1, X, body)

        def rest(d):
            chip = lax.rem(x + X - d, X)
            l = 2 * chip + 1 - c

            @pl.when(jnp.where(chip == x, own(l), cross(l, chip, x)))
            def _():
                over(buf, ps, arrivals, l).wait_recv()
        loop(0, X, rest)

    def spread_done(buf, xs, ps, arrivals, cross, own):
        def body(d):
            chip = lax.rem(x + d, X)

            @pl.when(cross(i, x, chip))
            def _():
                across(buf, xs, arrivals, chip).wait_send()
            source = lax.rem(x + X - d, X)
            l = 2 * source + c

            @pl.when(cross(l, source, x))
            def _():
                over(buf, ps, arrivals, l).wait_send()
        loop(1, X, body)

        @pl.when(own(i))
        def _():
            over(buf, ps, arrivals, i).wait_send()

    def core_copy(n, chip):
        return copy(S.at[chip], T1.at[n, chip], s1.at[chip], q1.at[n, chip], row=mate)

    def chip_copy(n, chip, slot):
        return copy(A.at[chip], T2.at[n, slot], s2.at[chip], q2.at[n, slot], row=2 * chip + c)

    def sum_first(n, partial, into):
        def body(d):
            chip = lax.rem(x + d, X)

            @pl.when(into(x, chip))
            def _():
                partial(S.at[chip], 2 * chip + 1 - c)
                core_copy(n, chip).start()
                partial(A.at[chip], 2 * chip + c)
        loop(1, X + 1, body)

    def sum_second(n, into):
        def body(d):
            chip = lax.rem(x + d, X)

            @pl.when(into(x, chip))
            def _():
                core_copy(n, chip).wait_recv()
                A[chip] = A[chip] + T1[n, chip]

                @pl.when(chip != x)
                def _():
                    chip_copy(n, chip, x).start()
        loop(1, X + 1, body)

    def sum_last(n, out, into, sign):
        total = A.at[x]

        def body(d):
            chip = lax.rem(x + d, X)

            @pl.when(into(chip, x))
            def _():
                chip_copy(n, chip, chip).wait_recv()
                total[...] = total[...] + T2[n, chip]
        loop(1, X, body)
        out[...] = total[...] if sign > 0 else 0.0 - total[...]

        def sent(d):
            chip = lax.rem(x + d, X)

            @pl.when(into(x, chip))
            def _():
                core_copy(n, chip).wait_send()

                @pl.when(chip != x)
                def _():
                    chip_copy(n, chip, x).wait_send()
        loop(1, X + 1, sent)

    every = C - 1
    M_line = (Mb, m_s, m_r)
    R_line = (Rb, r_s, r_r)
    N_line = (Nr, n_s, n_r)
    Y_line = (Yb, y_s, y_r)
    N_col = (Nc, c_x, c_p, c_r, lambda l, a, b: l >= j, lambda l: l >= j)
    X_col = (Xc, x_x, x_p, x_r, lambda l, a, b: a < b, lambda l: lax.rem(l, 2) == 0)

    Mb[j] = panel[...] * mask[...]
    pass_on(*M_line, 0, every, every, False)
    Nc[i] = node[...]
    spread(*N_col)

    @when(c == 0, j != i + 1)
    def _():
        Rb[i + 1] = jnp.zeros(root.shape, F32)
    Rb[j] = root[...]
    pass_on(*R_line, 0, i, every, True)
    collect(*N_col)

    @pl.when(j <= k)
    def _():
        Nr[j] = Nc[k]
    pass_on(*N_line, 0, k, k, True)

    multiply(Xc.at[i], Mb.at[j], Nc.at[j], False, False)

    def arrive(r):
        pass_on(*M_line, r, every, every, False)
        pass_on(*R_line, r, i, every, True)
        pass_on(*N_line, r, k, k, True)

        @pl.when(j + r < C)
        def _():
            multiply(Xc.at[i], Mb.at[j + r], Nc.at[j + r], False, True)
    loop(1, C, arrive)
    spread(*X_col)

    below = lambda a, b: b <= a
    sum_first(0, lambda dst, t: multiply(dst, Rb.at[t], Rb.at[j], True, False), below)
    sum_second(0, below)
    collect(*X_col)

    multiply(Yb.at[j], Rb.at[0], Xc.at[0], False, False)
    loop(1, i + 1, lambda t: multiply(Yb.at[j], Rb.at[t], Xc.at[t], False, True))
    pass_on(*Y_line, 0, every, every, True)
    sum_last(0, out_rr, below, 1)

    sum_first(1, lambda dst, t: multiply(dst, Rb.at[t], Yb.at[j], True, False), below)
    sum_second(1, below)
    loop(1, C, lambda r: pass_on(*Y_line, r, every, every, True))
    sum_last(1, out_or, below, -1)

    def node_part(dst, t):
        multiply(dst, Yb.at[t], Yb.at[j], True, False)

        @when(t <= k, j <= k)
        def _():
            multiply(dst, Nr.at[t], Nr.at[j], True, True)
    always = lambda a, b: a >= 0
    sum_first(2, node_part, always)
    sum_second(2, always)
    sum_last(2, out_nn, always, 1)

    sent_on(*M_line, every, every, False)
    sent_on(*R_line, i, every, True)
    sent_on(*N_line, k, k, True)
    sent_on(*Y_line, every, every, True)
    spread_done(*N_col)
    spread_done(*X_col)


def shards(R, C, root_inverse, panel, node_inverse, structure):
    B = root_inverse.shape[0]
    X = R // 2
    mask = jnp.repeat(structure, BS).astype(F32)[:, None]
    block = jax.ShapeDtypeStruct((B, B), F32)
    dma = pltpu.SemaphoreType.DMA
    slots = lambda *n: pltpu.VMEM(n + (B, B), F32)
    vmem = pl.BlockSpec(memory_space=pltpu.VMEM)
    return pl.pallas_call(
        functools.partial(kernel, R, C),
        out_shape=(block, block, block),
        in_specs=[vmem] * 4,
        out_specs=(vmem,) * 3,
        scratch_shapes=[
            slots(C), slots(C), slots(C), slots(R), slots(R), slots(C),
            slots(X), slots(X), slots(3, X), slots(3, X),
        ] + [dma((2, C)), dma((C,))] * 4 + [dma((X,)), dma((R,)), dma((R,))] * 2 + [
            dma((X,)), dma((3, X)), dma((X,)), dma((3, X)),
        ],
        compiler_params=pltpu.CompilerParams(
            collective_id=0, has_side_effects=True, vmem_limit_bytes=60 * 2**20),
    )(root_inverse, panel, node_inverse, mask)


def solution(mesh):
    placed = (
        P(("grp", "row"), "col"),
        P(("grp", "row"), "col"),
        P(("grp", "row"), "col"),
        P(("grp", "row")),
    )
    return jax.shard_map(
        functools.partial(shards, mesh.shape["row"], mesh.shape["col"]),
        mesh=mesh,
        in_specs=placed,
        out_specs=(P(("grp", "row"), "col"), P(("grp", "row"), "col"), P(("grp", "row"), "col")),
        check_vma=False,
    )
```

time: 599 us -> 272 us (0.45)
  waiting for transfers between devices: 529 us -> 0 us
  Pallas kernels: 0 us -> 260 us
  matrix products: 49.7 us -> 0 us
  between operations: 13.9 us -> 0.65 us
    all_gather x7 -> x0, waiting for transfers between devices: 444 us -> none  [the longest x1 81.4 us: shards(): lax.all_gather(sigma_root, 'col', axis=1, tiled=True)]
    pallas_call x0 -> x1, Pallas kernels: none -> 260 us  [shards(): pl.pallas_call(functools.partial(kernel, R, C), out_shape=(block, block,...]
    reduce_scatter x2 -> x0, waiting for transfers between devices: 82 us -> none  [the longest x1 44.8 us: shards(): lax.psum_scatter(product(node_rows.T, node_inverse) - product(scaled_full...]
    dot_general x5 -> x0, matrix products: 49.7 us -> none  [product(): jnp.dot(left_side, right_side, precision=PRECISE, preferred_element_type=...]
  transfers between devices with their start and end apart: 9 -> 0, of which waited for: 9 -> 0; matrix products, arithmetic and copies ran while one was open for 7% -> 0% of each run, Pallas kernels for 0% -> 0%
where the time goes in v1:
time: 272 us; the launch traced here: 268 us
  Pallas kernels  260 us (96%)
  local copies, waits for them, and re-layouts  5.91 us (2%)
    pallas_call x1, Pallas kernels, shards(): pl.pallas_call(functools.partial(kernel, R, C), out_shape=(block, block,...  260 us

profile of v1, /device:TPU:26, one launch (start us, length us, event | category | flops | bytes accessed | tf_op | source)
XLA Modules:
  0.0 267.7 jit_solution(12707385314787306558)
XLA Ops:
  0.6 0.7 convert_element_type.14
  1.3 0.1 broadcast_in_dim.4
  1.4 0.9 convert_element_type.16.mask
  2.3 260.5 %shard_map.67 = (f32[512,512]{1,0:T(8,128)}, f32[512,512]{1,0:T(8,128)}, f32[512,512]{1,0:T(8,128)}) custom-call(f32[512,512]{1,0:T(8,128)} %root.1, f32[512,512]{1,0:T(8,128)} %panel.1, f32[512,512]{1,0:T(8,128)} %node.1, f32[512,1]{1,0:T(8,128)} %convert_element_type.16.mask), custom_call_target="tpu_custom_call" | custom-call | tf_op jit(solution)/shard_map/pallas_call | solution.py:325
  262.8 0.0 copy-start.1
  262.8 2.4 copy.11
  265.1 0.0 copy-done.1
  265.1 0.0 copy-start
  265.1 1.0 copy.12
  266.1 0.6 copy-done
  266.7 1.0 copy.13
Async XLA Ops:
  262.8 2.4 copy-start.1
  265.1 1.6 copy-start

commit v2 on v1

--- a/solution.py
+++ b/solution.py
@@ -39,9 +39,9 @@
 
 
 def kernel(R, C, root, panel, node, mask, out_rr, out_or, out_nn,
-           Mb, Rb, Nr, Nc, Xc, Yb, S, A, T1, T2,
+           Mb, Rb, Nr, Nc, N0, X0, Xc, Yb, S, A, T1, T2,
            m_s, m_r, r_s, r_r, n_s, n_r, y_s, y_r,
-           c_x, c_p, c_r, x_x, x_p, x_r, s1, q1, s2, q2):
+           c_x, c_p, c_r, d_x, d_p, d_r, x_x, x_p, x_r, s1, q1, s2, q2, h_s, h_r):
     X = R // 2
     i, j = lax.axis_index("row"), lax.axis_index("col")
     x, c = i // 2, lax.rem(i, 2)
@@ -90,15 +90,15 @@
     def to_right(buf, sends, arrivals, l):
         return copy(buf.at[l], buf.at[l], sends.at[1, l], arrivals.at[l], col=right)
 
-    def pass_on(buf, sends, arrivals, r, top, end, go_right):
+    def pass_on(buf, sends, arrivals, r, top, end, go_right, low=0):
         l = j + r
 
-        @when(l <= top, l < C, j <= end)
+        @when(l <= top, l < C, j <= end, j >= low)
         def _():
             if not (isinstance(r, int) and r == 0):
                 to_left(buf, sends, arrivals, l).wait_recv()
 
-            @pl.when(j > 0)
+            @pl.when(j > low)
             def _():
                 to_left(buf, sends, arrivals, l).start()
 
@@ -114,11 +114,11 @@
                 def _():
                     to_right(buf, sends, arrivals, m).start()
 
-    def sent_on(buf, sends, arrivals, top, end, go_right):
+    def sent_on(buf, sends, arrivals, top, end, go_right, low=0):
         def body(r):
             l, m = j + r, j - r
 
-            @when(l <= top, l < C, j <= end, j > 0)
+            @when(l <= top, l < C, j <= end, j > low)
             def _():
                 to_left(buf, sends, arrivals, l).wait_send()
 
@@ -248,18 +248,41 @@
     N_line = (Nr, n_s, n_r)
     Y_line = (Yb, y_s, y_r)
     N_col = (Nc, c_x, c_p, c_r, lambda l, a, b: l >= j, lambda l: l >= j)
+    N0_col = (N0, d_x, d_p, d_r, lambda l, a, b: l >= 0, lambda l: l >= 0)
     X_col = (Xc, x_x, x_p, x_r, lambda l, a, b: a < b, lambda l: lax.rem(l, 2) == 0)
 
-    Mb[j] = panel[...] * mask[...]
-    pass_on(*M_line, 0, every, every, False)
+    def node_hop():
+        return copy(Nc.at[i], N0.at[i], h_s.at[0], h_r.at[0], col=right)
+
+    def panel_hop():
+        return copy(Mb.at[0], Mb.at[0], h_s.at[1], h_r.at[1], col=right)
+
+    def scaled_hop():
+        return copy(X0, Xc.at[i], h_s.at[2], h_r.at[2], col=left)
+
     Nc[i] = node[...]
     spread(*N_col)
+
+    @pl.when(j == 0)
+    def _():
+        node_hop().start()
+    Mb[j] = panel[...] * mask[...]
+
+    @pl.when(j == 0)
+    def _():
+        panel_hop().start()
+    pass_on(*M_line, 0, every, every, False, 1)
 
     @when(c == 0, j != i + 1)
     def _():
         Rb[i + 1] = jnp.zeros(root.shape, F32)
     Rb[j] = root[...]
     pass_on(*R_line, 0, i, every, True)
+
+    @pl.when(j == 1)
+    def _():
+        node_hop().wait_recv()
+        spread(*N0_col)
     collect(*N_col)
 
     @pl.when(j <= k)
@@ -267,17 +290,38 @@
         Nr[j] = Nc[k]
     pass_on(*N_line, 0, k, k, True)
 
-    multiply(Xc.at[i], Mb.at[j], Nc.at[j], False, False)
+    @pl.when(j == 1)
+    def _():
+        collect(*N0_col)
+        panel_hop().wait_recv()
+        multiply(X0, Mb.at[0], N0.at[0], False, False)
+        multiply(X0, Mb.at[1], N0.at[1], False, True)
+
+    @pl.when(j > 0)
+    def _():
+        multiply(Xc.at[i], Mb.at[j], Nc.at[j], False, False)
 
     def arrive(r):
-        pass_on(*M_line, r, every, every, False)
+        pass_on(*M_line, r, every, every, False, 1)
+
+        @when(j == 1, j + r < C)
+        def _():
+            multiply(X0, Mb.at[j + r], N0.at[j + r], False, True)
+
+            @pl.when(j + r == C - 1)
+            def _():
+                scaled_hop().start()
         pass_on(*R_line, r, i, every, True)
         pass_on(*N_line, r, k, k, True)
 
-        @pl.when(j + r < C)
+        @when(j > 0, j + r < C)
         def _():
             multiply(Xc.at[i], Mb.at[j + r], Nc.at[j + r], False, True)
     loop(1, C, arrive)
+
+    @pl.when(j == 0)
+    def _():
+        scaled_hop().wait_recv()
     spread(*X_col)
 
     below = lambda a, b: b <= a
@@ -306,7 +350,17 @@
     sum_second(2, always)
     sum_last(2, out_nn, always, 1)
 
-    sent_on(*M_line, every, every, False)
+    sent_on(*M_line, every, every, False, 1)
+
+    @pl.when(j == 0)
+    def _():
+        node_hop().wait_send()
+        panel_hop().wait_send()
+
+    @pl.when(j == 1)
+    def _():
+        scaled_hop().wait_send()
+        spread_done(*N0_col)
     sent_on(*R_line, i, every, True)
     sent_on(*N_line, k, k, True)
     sent_on(*Y_line, every, every, True)
@@ -328,10 +382,10 @@
         in_specs=[vmem] * 4,
         out_specs=(vmem,) * 3,
         scratch_shapes=[
-            slots(C), slots(C), slots(C), slots(R), slots(R), slots(C),
+            slots(C), slots(C), slots(C), slots(R), slots(R), slots(), slots(R), slots(C),
             slots(X), slots(X), slots(3, X), slots(3, X),
-        ] + [dma((2, C)), dma((C,))] * 4 + [dma((X,)), dma((R,)), dma((R,))] * 2 + [
-            dma((X,)), dma((3, X)), dma((X,)), dma((3, X)),
+        ] + [dma((2, C)), dma((C,))] * 4 + [dma((X,)), dma((R,)), dma((R,))] * 3 + [
+            dma((X,)), dma((3, X)), dma((X,)), dma((3, X)), dma((3,)), dma((3,)),
         ],
         compiler_params=pltpu.CompilerParams(
             collective_id=0, has_side_effects=True, vmem_limit_bytes=60 * 2**20),

time: 272 us -> 269 us (0.989)
  Pallas kernels: 260 us -> 256 us
    pallas_call x1, Pallas kernels: 260 us -> 256 us  [shards(): pl.pallas_call(functools.partial(kernel, R, C), out_shape=(block, block,...]
where the time goes in v2:
time: 269 us; the launch traced here: 263 us
  Pallas kernels  256 us (95%)
  local copies, waits for them, and re-layouts  5.91 us (2%)
    pallas_call x1, Pallas kernels, shards(): pl.pallas_call(functools.partial(kernel, R, C), out_shape=(block, block,...  256 us

profile of v2, /device:TPU:26, one launch (start us, length us, event | category | flops | bytes accessed | tf_op | source)
XLA Modules:
  0.0 263.4 jit_solution(4544579528392250621)
XLA Ops:
  0.6 0.7 convert_element_type.14
  1.3 0.1 broadcast_in_dim.4
  1.4 0.9 convert_element_type.16.mask
  2.3 256.1 %shard_map.67 = (f32[512,512]{1,0:T(8,128)}, f32[512,512]{1,0:T(8,128)}, f32[512,512]{1,0:T(8,128)}) custom-call(f32[512,512]{1,0:T(8,128)} %root.1, f32[512,512]{1,0:T(8,128)} %panel.1, f32[512,512]{1,0:T(8,128)} %node.1, f32[512,1]{1,0:T(8,128)} %convert_element_type.16.mask), custom_call_target="tpu_custom_call" | custom-call | tf_op jit(solution)/shard_map/pallas_call | solution.py:379
  258.4 0.0 copy-start.1
  258.4 2.4 copy.11
  260.8 0.0 copy-done.1
  260.8 0.0 copy-start
  260.8 1.0 copy.12
  261.8 0.6 copy-done
  262.4 1.0 copy.13
Async XLA Ops:
  258.4 2.4 copy-start.1
  260.8 1.6 copy-start

commit v3 on v2

--- a/solution.py
+++ b/solution.py
@@ -8,6 +8,7 @@
 from jax.sharding import PartitionSpec as P
 
 BS = 64
+Q = 2
 MESH = pl.DeviceIdType.MESH
 F32, BF16 = jnp.float32, jnp.bfloat16
 
@@ -84,23 +85,32 @@
     loop(1, X, lambda d: greet(2 * lax.rem(x + d, X) + c, j))
     pl.semaphore_wait(barrier, X + jnp.where(j > 0, 1, 0) + jnp.where(j < C - 1, 1, 0))
 
-    def to_left(buf, sends, arrivals, l):
-        return copy(buf.at[l], buf.at[l], sends.at[0, l], arrivals.at[l], col=left)
+    H = root.shape[0] // Q
+
+    def rows(q):
+        return pl.ds(q * H, H)
+
+    def part(buf, l, q):
+        return buf.at[l] if q is None else buf.at[l, rows(q)]
+
+    def to_left(buf, sends, arrivals, l, q=None):
+        ref, n = part(buf, l, q), l + C * (q or 0)
+        return copy(ref, ref, sends.at[0, n], arrivals.at[n], col=left)
 
     def to_right(buf, sends, arrivals, l):
         return copy(buf.at[l], buf.at[l], sends.at[1, l], arrivals.at[l], col=right)
 
-    def pass_on(buf, sends, arrivals, r, top, end, go_right, low=0):
+    def pass_on(buf, sends, arrivals, r, top, end, go_right, low=0, q=None):
         l = j + r
 
         @when(l <= top, l < C, j <= end, j >= low)
         def _():
             if not (isinstance(r, int) and r == 0):
-                to_left(buf, sends, arrivals, l).wait_recv()
+                to_left(buf, sends, arrivals, l, q).wait_recv()
 
             @pl.when(j > low)
             def _():
-                to_left(buf, sends, arrivals, l).start()
+                to_left(buf, sends, arrivals, l, q).start()
 
         if go_right:
             m = j - r
@@ -114,13 +124,13 @@
                 def _():
                     to_right(buf, sends, arrivals, m).start()
 
-    def sent_on(buf, sends, arrivals, top, end, go_right, low=0):
+    def sent_on(buf, sends, arrivals, top, end, go_right, low=0, q=None):
         def body(r):
             l, m = j + r, j - r
 
             @when(l <= top, l < C, j <= end, j > low)
             def _():
-                to_left(buf, sends, arrivals, l).wait_send()
+                to_left(buf, sends, arrivals, l, q).wait_send()
 
             if go_right:
                 @when(m >= 0, m <= top, j <= end, j < C - 1, j < end)
@@ -128,34 +138,36 @@
                     to_right(buf, sends, arrivals, m).wait_send()
         loop(0, C, body)
 
-    def across(buf, sems, arrivals, d_chip):
-        return copy(buf.at[i], buf.at[i], sems.at[d_chip], arrivals.at[i], row=2 * d_chip + c)
-
-    def over(buf, sems, arrivals, l):
-        return copy(buf.at[l], buf.at[l], sems.at[l], arrivals.at[l], row=mate)
-
-    def spread(buf, xs, ps, arrivals, cross, own):
+    def across(buf, sems, arrivals, d_chip, q):
+        ref, n = part(buf, i, q), q or 0
+        return copy(ref, ref, sems.at[d_chip + X * n], arrivals.at[i + R * n], row=2 * d_chip + c)
+
+    def over(buf, sems, arrivals, l, q):
+        ref, n = part(buf, l, q), l + R * (q or 0)
+        return copy(ref, ref, sems.at[n], arrivals.at[n], row=mate)
+
+    def spread(buf, xs, ps, arrivals, cross, own, q=None):
         def body(d):
             chip = lax.rem(x + d, X)
 
             @pl.when(cross(i, x, chip))
             def _():
-                across(buf, xs, arrivals, chip).start()
+                across(buf, xs, arrivals, chip, q).start()
         loop(1, X, body)
 
         @pl.when(own(i))
         def _():
-            over(buf, ps, arrivals, i).start()
-
-    def collect(buf, xs, ps, arrivals, cross, own):
+            over(buf, ps, arrivals, i, q).start()
+
+    def collect(buf, xs, ps, arrivals, cross, own, q=None):
         def body(d):
             chip = lax.rem(x + X - d, X)
             l = 2 * chip + c
 
             @pl.when(cross(l, chip, x))
             def _():
-                over(buf, ps, arrivals, l).wait_recv()
-                over(buf, ps, arrivals, l).start()
+                over(buf, ps, arrivals, l, q).wait_recv()
+                over(buf, ps, arrivals, l, q).start()
         loop(1, X, body)
 
         def rest(d):
@@ -164,27 +176,27 @@
 
             @pl.when(jnp.where(chip == x, own(l), cross(l, chip, x)))
             def _():
-                over(buf, ps, arrivals, l).wait_recv()
+                over(buf, ps, arrivals, l, q).wait_recv()
         loop(0, X, rest)
 
-    def spread_done(buf, xs, ps, arrivals, cross, own):
+    def spread_done(buf, xs, ps, arrivals, cross, own, q=None):
         def body(d):
             chip = lax.rem(x + d, X)
 
             @pl.when(cross(i, x, chip))
             def _():
-                across(buf, xs, arrivals, chip).wait_send()
+                across(buf, xs, arrivals, chip, q).wait_send()
             source = lax.rem(x + X - d, X)
             l = 2 * source + c
 
             @pl.when(cross(l, source, x))
             def _():
-                over(buf, ps, arrivals, l).wait_send()
+                over(buf, ps, arrivals, l, q).wait_send()
         loop(1, X, body)
 
         @pl.when(own(i))
         def _():
-            over(buf, ps, arrivals, i).wait_send()
+            over(buf, ps, arrivals, i, q).wait_send()
 
     def core_copy(n, chip):
         return copy(S.at[chip], T1.at[n, chip], s1.at[chip], q1.at[n, chip], row=mate)
@@ -254,89 +266,94 @@
     def node_hop():
         return copy(Nc.at[i], N0.at[i], h_s.at[0], h_r.at[0], col=right)
 
-    def panel_hop():
-        return copy(Mb.at[0], Mb.at[0], h_s.at[1], h_r.at[1], col=right)
-
-    def scaled_hop():
-        return copy(X0, Xc.at[i], h_s.at[2], h_r.at[2], col=left)
+    def panel_hop(q):
+        return copy(part(Mb, 0, q), part(Mb, 0, q), h_s.at[1 + q], h_r.at[1 + q], col=right)
+
+    def scaled_hop(q):
+        n = 1 + Q + q
+        return copy(X0.at[rows(q)], part(Xc, i, q), h_s.at[n], h_r.at[n], col=left)
 
     Nc[i] = node[...]
-    spread(*N_col)
 
     @pl.when(j == 0)
     def _():
         node_hop().start()
     Mb[j] = panel[...] * mask[...]
-
-    @pl.when(j == 0)
-    def _():
-        panel_hop().start()
-    pass_on(*M_line, 0, every, every, False, 1)
+    for q in range(Q):
+        @pl.when(j == 0)
+        def _():
+            panel_hop(q).start()
+        pass_on(*M_line, 0, every, every, False, 1, q)
+    spread(*N_col)
 
     @when(c == 0, j != i + 1)
     def _():
         Rb[i + 1] = jnp.zeros(root.shape, F32)
     Rb[j] = root[...]
     pass_on(*R_line, 0, i, every, True)
+    collect(*N_col)
 
     @pl.when(j == 1)
     def _():
         node_hop().wait_recv()
         spread(*N0_col)
-    collect(*N_col)
-
-    @pl.when(j <= k)
-    def _():
-        Nr[j] = Nc[k]
-    pass_on(*N_line, 0, k, k, True)
-
-    @pl.when(j == 1)
-    def _():
-        collect(*N0_col)
-        panel_hop().wait_recv()
-        multiply(X0, Mb.at[0], N0.at[0], False, False)
-        multiply(X0, Mb.at[1], N0.at[1], False, True)
-
-    @pl.when(j > 0)
-    def _():
-        multiply(Xc.at[i], Mb.at[j], Nc.at[j], False, False)
+
+    def scaled_part(dst, blocks, low, q):
+        multiply(dst, part(Mb, low, q), blocks.at[low], False, False)
+        loop(low + 1, C, lambda l: multiply(dst, part(Mb, l, q), blocks.at[l], False, True))
+
+    for q in range(Q):
+        loop(1, C, lambda r: pass_on(*M_line, r, every, every, False, 1, q))
+
+        @pl.when(j == 1)
+        def _():
+            if q == 0:
+                collect(*N0_col)
+            panel_hop(q).wait_recv()
+            scaled_part(X0.at[rows(q)], N0, 0, q)
+            scaled_hop(q).start()
+
+        @pl.when(j > 0)
+        def _():
+            scaled_part(part(Xc, i, q), Nc, j, q)
+            spread(*X_col, q)
+        if q == 0:
+            pass_on(*R_line, 1, i, every, True)
+
+            @pl.when(j <= k)
+            def _():
+                Nr[j] = Nc[k]
+            pass_on(*N_line, 0, k, k, True)
+
+    for q in range(Q):
+        @pl.when(j == 0)
+        def _():
+            scaled_hop(q).wait_recv()
+            spread(*X_col, q)
 
     def arrive(r):
-        pass_on(*M_line, r, every, every, False, 1)
-
-        @when(j == 1, j + r < C)
-        def _():
-            multiply(X0, Mb.at[j + r], N0.at[j + r], False, True)
-
-            @pl.when(j + r == C - 1)
-            def _():
-                scaled_hop().start()
-        pass_on(*R_line, r, i, every, True)
+        @pl.when(r > 1)
+        def _():
+            pass_on(*R_line, r, i, every, True)
         pass_on(*N_line, r, k, k, True)
-
-        @when(j > 0, j + r < C)
-        def _():
-            multiply(Xc.at[i], Mb.at[j + r], Nc.at[j + r], False, True)
     loop(1, C, arrive)
 
-    @pl.when(j == 0)
-    def _():
-        scaled_hop().wait_recv()
-    spread(*X_col)
+    for q in range(Q):
+        collect(*X_col, q)
+
+    multiply(Yb.at[j], Rb.at[0], Xc.at[0], False, False)
+    loop(1, i + 1, lambda t: multiply(Yb.at[j], Rb.at[t], Xc.at[t], False, True))
+    pass_on(*Y_line, 0, every, every, True)
 
     below = lambda a, b: b <= a
     sum_first(0, lambda dst, t: multiply(dst, Rb.at[t], Rb.at[j], True, False), below)
     sum_second(0, below)
-    collect(*X_col)
-
-    multiply(Yb.at[j], Rb.at[0], Xc.at[0], False, False)
-    loop(1, i + 1, lambda t: multiply(Yb.at[j], Rb.at[t], Xc.at[t], False, True))
-    pass_on(*Y_line, 0, every, every, True)
+    loop(1, C // 2, lambda r: pass_on(*Y_line, r, every, every, True))
     sum_last(0, out_rr, below, 1)
 
     sum_first(1, lambda dst, t: multiply(dst, Rb.at[t], Yb.at[j], True, False), below)
     sum_second(1, below)
-    loop(1, C, lambda r: pass_on(*Y_line, r, every, every, True))
+    loop(C // 2, C, lambda r: pass_on(*Y_line, r, every, every, True))
     sum_last(1, out_or, below, -1)
 
     def node_part(dst, t):
@@ -350,22 +367,25 @@
     sum_second(2, always)
     sum_last(2, out_nn, always, 1)
 
-    sent_on(*M_line, every, every, False, 1)
+    for q in range(Q):
+        sent_on(*M_line, every, every, False, 1, q)
+        spread_done(*X_col, q)
 
     @pl.when(j == 0)
     def _():
         node_hop().wait_send()
-        panel_hop().wait_send()
+        for q in range(Q):
+            panel_hop(q).wait_send()
 
     @pl.when(j == 1)
     def _():
-        scaled_hop().wait_send()
+        for q in range(Q):
+            scaled_hop(q).wait_send()
         spread_done(*N0_col)
     sent_on(*R_line, i, every, True)
     sent_on(*N_line, k, k, True)
     sent_on(*Y_line, every, every, True)
     spread_done(*N_col)
-    spread_done(*X_col)
 
 
 def shards(R, C, root_inverse, panel, node_inverse, structure):
@@ -384,8 +404,8 @@
         scratch_shapes=[
             slots(C), slots(C), slots(C), slots(R), slots(R), slots(), slots(R), slots(C),
             slots(X), slots(X), slots(3, X), slots(3, X),
-        ] + [dma((2, C)), dma((C,))] * 4 + [dma((X,)), dma((R,)), dma((R,))] * 3 + [
-            dma((X,)), dma((3, X)), dma((X,)), dma((3, X)), dma((3,)), dma((3,)),
+        ] + [dma((2, Q * C)), dma((Q * C,))] * 4 + [dma((Q * X,)), dma((Q * R,)), dma((Q * R,))] * 3 + [
+            dma((X,)), dma((3, X)), dma((X,)), dma((3, X)), dma((1 + 2 * Q,)), dma((1 + 2 * Q,)),
         ],
         compiler_params=pltpu.CompilerParams(
             collective_id=0, has_side_effects=True, vmem_limit_bytes=60 * 2**20),

time: 269 us -> 272 us (1.011); the launches traced: 263 us -> 272 us
  Pallas kernels: 256 us -> 265 us
    pallas_call x1, Pallas kernels: 256 us -> 265 us  [shards(): pl.pallas_call(functools.partial(kernel, R, C), out_shape=(block, block,...]
where the time goes in v3:
time: 272 us
  Pallas kernels  265 us (97%)
  local copies, waits for them, and re-layouts  5.91 us (2%)
    pallas_call x1, Pallas kernels, shards(): pl.pallas_call(functools.partial(kernel, R, C), out_shape=(block, block,...  265 us

profile of v3, /device:TPU:26, one launch (start us, length us, event | category | flops | bytes accessed | tf_op | source)
XLA Modules:
  0.0 272.2 jit_solution(11968930538352812574)
XLA Ops:
  0.6 0.7 convert_element_type.14
  1.3 0.1 broadcast_in_dim.4
  1.4 0.9 convert_element_type.16.mask
  2.3 265.0 %shard_map.67 = (f32[512,512]{1,0:T(8,128)}, f32[512,512]{1,0:T(8,128)}, f32[512,512]{1,0:T(8,128)}) custom-call(f32[512,512]{1,0:T(8,128)} %root.1, f32[512,512]{1,0:T(8,128)} %panel.1, f32[512,512]{1,0:T(8,128)} %node.1, f32[512,1]{1,0:T(8,128)} %convert_element_type.16.mask), custom_call_target="tpu_custom_call" | custom-call | tf_op jit(solution)/shard_map/pallas_call | solution.py:399
  267.3 0.0 copy-start.1
  267.3 2.4 copy.11
  269.6 0.0 copy-done.1
  269.6 0.0 copy-start
  269.6 1.0 copy.12
  270.6 0.6 copy-done
  271.2 1.0 copy.13
Async XLA Ops:
  267.3 2.4 copy-start.1
  269.6 1.6 copy-start

commit v4 on v3

--- a/solution.py
+++ b/solution.py
@@ -331,12 +331,7 @@
             scaled_hop(q).wait_recv()
             spread(*X_col, q)
 
-    def arrive(r):
-        @pl.when(r > 1)
-        def _():
-            pass_on(*R_line, r, i, every, True)
-        pass_on(*N_line, r, k, k, True)
-    loop(1, C, arrive)
+    loop(2, C, lambda r: pass_on(*R_line, r, i, every, True))
 
     for q in range(Q):
         collect(*X_col, q)
@@ -345,15 +340,19 @@
     loop(1, i + 1, lambda t: multiply(Yb.at[j], Rb.at[t], Xc.at[t], False, True))
     pass_on(*Y_line, 0, every, every, True)
 
+    def arrive(r):
+        pass_on(*N_line, r, k, k, True)
+        pass_on(*Y_line, r, every, every, True)
+
     below = lambda a, b: b <= a
     sum_first(0, lambda dst, t: multiply(dst, Rb.at[t], Rb.at[j], True, False), below)
     sum_second(0, below)
-    loop(1, C // 2, lambda r: pass_on(*Y_line, r, every, every, True))
+    loop(1, C // 2, arrive)
     sum_last(0, out_rr, below, 1)
 
     sum_first(1, lambda dst, t: multiply(dst, Rb.at[t], Yb.at[j], True, False), below)
     sum_second(1, below)
-    loop(C // 2, C, lambda r: pass_on(*Y_line, r, every, every, True))
+    loop(C // 2, C, arrive)
     sum_last(1, out_or, below, -1)
 
     def node_part(dst, t):

time: 272 us -> 256 us (0.941)
  Pallas kernels: 265 us -> 247 us
    pallas_call x1, Pallas kernels: 265 us -> 247 us  [shards(): pl.pallas_call(functools.partial(kernel, R, C), out_shape=(block, block,...]
where the time goes in v4:
time: 256 us; the launch traced here: 254 us
  Pallas kernels  247 us (96%)
  local copies, waits for them, and re-layouts  5.91 us (2%)
    pallas_call x1, Pallas kernels, shards(): pl.pallas_call(functools.partial(kernel, R, C), out_shape=(block, block,...  247 us

profile of v4, /device:TPU:26, one launch (start us, length us, event | category | flops | bytes accessed | tf_op | source)
XLA Modules:
  0.0 253.8 jit_solution(5253788511412568820)
XLA Ops:
  0.6 0.7 convert_element_type.14
  1.3 0.1 broadcast_in_dim.4
  1.4 0.9 convert_element_type.16.mask
  2.3 246.6 %shard_map.67 = (f32[512,512]{1,0:T(8,128)}, f32[512,512]{1,0:T(8,128)}, f32[512,512]{1,0:T(8,128)}) custom-call(f32[512,512]{1,0:T(8,128)} %root.1, f32[512,512]{1,0:T(8,128)} %panel.1, f32[512,512]{1,0:T(8,128)} %node.1, f32[512,1]{1,0:T(8,128)} %convert_element_type.16.mask), custom_call_target="tpu_custom_call" | custom-call | tf_op jit(solution)/shard_map/pallas_call | solution.py:398
  248.9 0.0 copy-start.1
  248.9 2.4 copy.11
  251.3 0.0 copy-done.1
  251.3 0.0 copy-start
  251.3 1.0 copy.12
  252.2 0.6 copy-done
  252.9 1.0 copy.13
Async XLA Ops:
  248.9 2.4 copy-start.1
  251.3 1.6 copy-start
